TPU v7x, 32 devices: a whole 2x2x4 slice. The times are simulated.
32 devices in a mesh: groups: 2 (over y), seq: 4 (over x, core), shard: 4 (over z).
Axes of the slice: x: 2, y: 2, z: 4, core: 2. Of those that a mesh axis runs over, the one named last changes fastest.
Arguments:
- qkv_img: bfloat16 [3, 8, 512, 2048], P(None, ('groups', 'shard'), 'seq'), parts along dimension 1, may hold values from -12 to 12
- qkv_txt: bfloat16 [3, 8, 64, 2048], P(None, ('groups', 'shard'), 'seq'), parts along dimension 1, may hold values from -8 to 8
- grad_img: bfloat16 [8, 512, 3072], P(('groups', 'shard'), 'seq'), parts along dimension 0, may hold values from -24 to 24
- grad_txt: bfloat16 [8, 64, 3072], P(('groups', 'shard'), 'seq'), parts along dimension 0, may hold values from -24 to 24
- out_w_img: bfloat16 [2048, 3072], P('seq', 'shard'), may hold values from -0.125 to 0.125
- out_w_txt: bfloat16 [2048, 3072], P('seq', 'shard'), may hold values from -0.125 to 0.125
Outputs:
- dqkv_img: bfloat16 [3, 8, 512, 2048], P(None, ('groups', 'shard'), 'seq'), parts along dimension 1
- dqkv_txt: bfloat16 [3, 8, 64, 2048], P(None, ('groups', 'shard'), 'seq'), parts along dimension 1
- dw_img: float32 [4096, 3072], P(('groups', 'seq'), 'shard'), parts along dimension 0
- dw_txt: float32 [4096, 3072], P(('groups', 'seq'), 'shard'), parts along dimension 0
There are 2 independent parts, one for each index of `groups`. A program takes and returns all parts, laid end to end along the dimension named above; an argument that names none is the same for every part. Nothing has to cross between parts.
All inputs are finite; a program needn't handle non-finite values.
Results may differ from a plain program's by a relative error of at most 0.0085.
Values may be sent and summed in bfloat16 or wider, within the bound.
A program may use at most 64 MiB of HBM per device.

v0:
```python
import jax
import jax.numpy as jnp
from jax import lax
from jax.sharding import PartitionSpec as P

HEAD_DIM = 128


def head_backward(query, keys, values, dout):
    scale = HEAD_DIM ** (-0.5)
    scores = jnp.dot(query, keys.T, preferred_element_type=jnp.float32) * scale
    top = jnp.max(scores, axis=-1, keepdims=True)
    expo = jnp.exp(scores - top)
    probs = expo / jnp.sum(expo, axis=-1, keepdims=True)
    probs_low = probs.astype(jnp.bfloat16)
    output = jnp.dot(probs_low, values, preferred_element_type=jnp.float32)
    dprobs = jnp.dot(dout, values.T, preferred_element_type=jnp.float32)
    delta = jnp.sum(dout.astype(jnp.float32) * output, axis=-1, keepdims=True)
    dscore = (probs * (dprobs - delta)).astype(jnp.bfloat16)
    dquery = (jnp.dot(dscore, keys, preferred_element_type=jnp.float32) * scale).astype(
        jnp.bfloat16
    )
    dkeys = (jnp.dot(dscore.T, query, preferred_element_type=jnp.float32) * scale).astype(
        jnp.bfloat16
    )
    dvalues = jnp.dot(probs_low.T, dout, preferred_element_type=jnp.float32).astype(jnp.bfloat16)
    return (output.astype(jnp.bfloat16), dquery, dkeys, dvalues)


def local(qkv_img, qkv_txt, grad_img, grad_txt, out_w_img, out_w_txt):
    heads_txt, heads_img = (
        lax.all_to_all(qkv_txt, "seq", split_axis=3, concat_axis=2, tiled=True),
        lax.all_to_all(qkv_img, "seq", split_axis=3, concat_axis=2, tiled=True),
    )
    weight_txt, weight_img = (
        lax.all_gather(out_w_txt, "shard", axis=1, tiled=True),
        lax.all_gather(out_w_img, "shard", axis=1, tiled=True),
    )
    full_txt, full_img = (
        lax.all_gather(grad_txt, "seq", axis=1, tiled=True),
        lax.all_gather(grad_img, "seq", axis=1, tiled=True),
    )
    cot_txt = full_txt[0]
    cot_img = full_img[0]
    text_len = cot_txt.shape[0]
    joint = jnp.concatenate([heads_txt[:, 0], heads_img[:, 0]], axis=1)
    total_len = joint.shape[1]
    local_width = joint.shape[2]
    head_count = local_width // HEAD_DIM
    dout = jnp.concatenate(
        [
            jnp.einsum("td,hd->th", cot_txt, weight_txt, preferred_element_type=jnp.float32),
            jnp.einsum("td,hd->th", cot_img, weight_img, preferred_element_type=jnp.float32),
        ],
        axis=0,
    ).astype(jnp.bfloat16)

    def arrange(block):
        return block.reshape(total_len, head_count, HEAD_DIM).transpose(1, 0, 2)

    def restore(block):
        return block.transpose(1, 0, 2).reshape(total_len, local_width)

    results = lax.map(
        lambda items: head_backward(*items),
        (arrange(joint[0]), arrange(joint[1]), arrange(joint[2]), arrange(dout)),
    )
    output = restore(results[0])
    grads = jnp.stack([restore(results[1]), restore(results[2]), restore(results[3])])
    back_txt = grads[:, None, :text_len]
    back_img = grads[:, None, text_len:]
    ret_txt, ret_img = (
        lax.all_to_all(back_txt, "seq", split_axis=2, concat_axis=3, tiled=True),
        lax.all_to_all(back_img, "seq", split_axis=2, concat_axis=3, tiled=True),
    )
    part_txt = jnp.dot(output[:text_len].T, cot_txt, preferred_element_type=jnp.float32)
    part_img = jnp.dot(output[text_len:].T, cot_img, preferred_element_type=jnp.float32)
    sum_txt, sum_img = (
        lax.psum_scatter(
            part_txt.astype(jnp.bfloat16), "shard", scatter_dimension=1, tiled=True
        ).astype(jnp.float32),
        lax.psum_scatter(
            part_img.astype(jnp.bfloat16), "shard", scatter_dimension=1, tiled=True
        ).astype(jnp.float32),
    )
    return (ret_img, ret_txt, sum_img, sum_txt)


def solution(mesh):
    return jax.shard_map(
        local,
        mesh=mesh,
        in_specs=(
            P(None, ("groups", "shard"), "seq", None),
            P(None, ("groups", "shard"), "seq", None),
            P(("groups", "shard"), "seq", None),
            P(("groups", "shard"), "seq", None),
            P("seq", "shard"),
            P("seq", "shard"),
        ),
        out_specs=(
            P(None, ("groups", "shard"), "seq", None),
            P(None, ("groups", "shard"), "seq", None),
            P(("groups", "seq"), "shard"),
            P(("groups", "seq"), "shard"),
        ),
        check_vma=False,
    )
```

profile of v0, /device:TPU:0, one launch (start us, length us, event | category | flops | bytes accessed | tf_op | source)
XLA Modules:
  0.0 331.0 jit_solution(3192047598824396975)
XLA Ops:
  10.8 2.7 reshape.23
  13.4 4.2 %all-to-all-start = ((bf16[4,2,12288]{2,1,0:T(2,128)(2,1)}), bf16[4,2,12288]{2,1,0:T(2,128)(2,1)S(1)}, u32[]{:S(2)}, u32[]{:S(2)}) async-start(bf16[4,2,12288]{2,1,0:T(2,128)(2,1)} %reshape.23), calls=%async_computation | async-start | bytes 393216 | tf_op jit(solution)/shard_map/all_to_all | solution.py:32
  17.6 4.2 %copy.63 = bf16[3,1,128,2048]{2,0,1,3:T(4,128)(2,1)} copy(bf16[3,1,128,2048]{3,2,1,0:T(8,128)(2,1)} %param.8) | data formatting | bytes 3145728 | tf_op args[0]
  23.0 3.6 %all-to-all-start.1 = ((bf16[3,1,128,2048]{2,0,1,3:T(4,128)(2,1)}), bf16[3,1,128,2048]{2,0,1,3:T(4,128)(2,1)S(1)}, u32[]{:S(2)}, u32[]{:S(2)}) async-start(bf16[3,1,128,2048]{2,0,1,3:T(4,128)(2,1)} %copy.63), calls=%async_computation.1 | async-start | bytes 4194304 | tf_op jit(solution)/shard_map/all_to_all | solution.py:33
  26.7 28.5 %all_gather.12 = bf16[1,64,3072]{2,1,0:T(8,128)(2,1)S(1)} all-gather(bf16[1,16,3072]{2,1,0:T(8,128)(2,1)S(1)} %copy-done.2), channel_id=1, replica_groups=mesh['groups'=2,'seq'=4,'shard'=4] {'seq'}, dimensions={1}, use_global_device_ids=true | all-gather | bytes 491520 | tf_op jit(solution)/shard_map/all_gather | solution.py:40
  55.2 3.0 reshape.24
  58.2 3.1 copy.83
  62.7 1.7 copy.65
  65.4 1.6 reshape_squeeze.9
  67.6 8.2 %all-gather.4.cloned.1.call-done = bf16[512,3072]{1,0:T(8,128)(2,1)} async-done(((bf16[512,768]{1,0:T(8,128)(2,1)}), bf16[512,3072]{1,0:T(8,128)(2,1)}) %all-gather.4.cloned.1.call-update) | async-done | bytes 3145744 | tf_op jit(solution)/shard_map/all_gather | solution.py:36
  75.8 3.0 convolution_convert_fusion.3
  78.7 25.8 %all-gather.6.cloned.1.call-done = bf16[1,512,3072]{2,1,0:T(8,128)(2,1)} async-done(((bf16[1,128,3072]{2,1,0:T(8,128)(2,1)}), bf16[1,512,3072]{2,1,0:T(8,128)(2,1)}) %all-gather.6.cloned.1.call-update) | async-done | bytes 3145744 | tf_op jit(solution)/shard_map/all_gather | solution.py:41
  104.6 65.1 %all-gather.8.cloned.1.call-done = bf16[512,3072]{1,0:T(8,128)(2,1)} async-done(((bf16[512,768]{1,0:T(8,128)(2,1)}), bf16[512,3072]{1,0:T(8,128)(2,1)}) %all-gather.8.cloned.1.call-update) | async-done | bytes 3145744 | tf_op jit(solution)/shard_map/all_gather | solution.py:37
  169.7 4.7 %fusion.37 = bf16[512,4,128]{2,0,1:T(8,128)(2,1)S(1)} fusion(bf16[4,128,3072]{2,1,0:T(8,128)(2,1)} %bitcast.152, bf16[1,512,3072]{2,1,0:T(8,128)(2,1)} %all-gather.6.cloned.1.call-done), kind=kOutput, calls=%fused_computation.52 | convolution fusion | flops 1610874880 | bytes 6815744 | tf_op jit(solution)/shard_map/td,hd->th/dot_general | solution.py:53
  174.5 20.1 %while.16 = (s32[]{:T(128)}, bf16[4,576,128]{2,1,0:T(8,128)(2,1)S(1)}, bf16[4,576,128]{2,1,0:T(8,128)(2,1)}, bf16[4,576,128]{2,1,0:T(8,128)(2,1)}, bf16[4,576,12...) while((s32[]{:T(128)}, ...), condition=%wide.region_4.5_spmd, body=%wide.region_0.4_spmd.sunk | while | flops 514251072 | bytes 12271209 | solution.py:64
  195.1 5.4 %convolution_convert_fusion.2 = bf16[512,3072]{1,0:T(8,128)(2,1)} fusion(bf16[512,512]{0,1:T(8,128)(2,1)S(1)} %bitcast.150, bf16[1,512,3072]{2,1,0:T(8,128)(2,1)} %all-gather.6.cloned.1.call-done), kind=kOutput, calls=%fused_computation.43 | convolution fusion | flops 1612185600 | bytes 6815744 | tf_op jit(solution)/shard_map/dot_general | solution.py:77
  200.8 2.6 convolution_convert_fusion.1
  203.4 1.5 copy.69
  205.2 1.7 copy.70
  207.1 1.5 copy.71
  209.9 3.4 %all-to-all-start.3 = ((bf16[3,1,64,512]{3,0,1,2:T(4,128)(2,1)}), bf16[3,1,64,512]{3,0,1,2:T(4,128)(2,1)S(1)}, u32[]{:S(2)}, u32[]{:S(2)}) async-start(bf16[3,1,64,512]{3,0,1,2:T(4,128)(2,1)} %copy.75), calls=%async_computation.3 | async-start | bytes 524288 | tf_op jit(solution)/shard_map/all_to_all | solution.py:73
  213.4 2.7 copy.72
  216.1 3.2 all-to-all-done.3
  219.3 3.6 %all-to-all-start.2 = ((bf16[3,1,512,512]{3,0,1,2:T(4,128)(2,1)}), bf16[3,1,512,512]{3,0,1,2:T(4,128)(2,1)S(1)}, u32[]{:S(2)}, u32[]{:S(2)}) async-start(bf16[3,1,512,512]{3,0,1,2:T(4,128)(2,1)} %copy.72), calls=%async_computation.2 | async-start | bytes 4194304 | tf_op jit(solution)/shard_map/all_to_all | solution.py:74
  223.7 24.9 %all-to-all-done.2 = bf16[3,1,512,512]{3,0,1,2:T(4,128)(2,1)S(1)} async-done(((bf16[3,1,512,512]{3,0,1,2:T(4,128)(2,1)}), bf16[3,1,512,512]{3,0,1,2:T(4,128)(2,1)S(1)}, u32[]{:S(2)}, u32[]{:S(2)}) %all-to-all-start.2) | async-done | bytes 1572896 | tf_op jit(solution)/shard_map/all_to_all | solution.py:74
  248.6 1.5 copy.73
  250.1 1.9 copy.74
  252.0 1.6 copy.80
  253.6 6.0 %reduce-scatter.3.cloned.1.call-done = bf16[512,768]{1,0:T(8,128)(2,1)} async-done(((bf16[512,3072]{1,0:T(8,128)(2,1)}), bf16[512,768]{1,0:T(8,128)(2,1)}) %reduce-scatter.3.cloned.1.call-update) | async-done | bytes 786448 | tf_op jit(solution)/shard_map/reduce_scatter | solution.py:82
  259.6 2.4 convert_element_type.36
  262.0 60.1 %reduce-scatter.5.cloned.1.call-done = bf16[512,768]{1,0:T(8,128)(2,1)} async-done(((bf16[512,3072]{1,0:T(8,128)(2,1)}), bf16[512,768]{1,0:T(8,128)(2,1)}) %reduce-scatter.5.cloned.1.call-update) | async-done | bytes 786448 | tf_op jit(solution)/shard_map/reduce_scatter | solution.py:79
  322.1 2.4 convert_element_type.38
  (82 shorter events, 31.0 us)
Async XLA Ops:
  7.2 2.2 copy-start.1
  7.2 68.6 %all-gather.4.cloned.1.call-start = ((), (), s32[]{:S(2)}) async-start(), calls=%async_computation.6 | async-start | bytes 3932160 | tf_op jit(solution)/shard_map/all_gather | solution.py:36
  7.9 96.7 %all-gather.6.cloned.1.call-start = ((), (), s32[]{:S(2)}) async-start(), calls=%async_computation.7 | async-start | bytes 3932160 | tf_op jit(solution)/shard_map/all_gather | solution.py:41
  8.7 161.0 %all-gather.8.cloned.1.call-start = ((), (), s32[]{:S(2)}) async-start(), calls=%async_computation.8 | async-start | bytes 3932160 | tf_op jit(solution)/shard_map/all_gather | solution.py:37
  13.4 9.5 %all-to-all-start = ((bf16[4,2,12288]{2,1,0:T(2,128)(2,1)}), bf16[4,2,12288]{2,1,0:T(2,128)(2,1)S(1)}, u32[]{:S(2)}, u32[]{:S(2)}) async-start(bf16[4,2,12288]{2,1,0:T(2,128)(2,1)} %reshape.23), calls=%async_computation | async-start | bytes 393216 | tf_op jit(solution)/shard_map/all_to_all | solution.py:32
  21.8 4.8 %copy-start.2 = (bf16[1,16,3072]{2,1,0:T(8,128)(2,1)S(1)}, bf16[1,16,3072]{2,1,0:T(8,128)(2,1)}, u32[]{:S(2)}) copy-start(bf16[1,16,3072]{2,1,0:T(8,128)(2,1)} %param.11) | copy-start | bytes 294916
  23.0 38.4 %all-to-all-start.1 = ((bf16[3,1,128,2048]{2,0,1,3:T(4,128)(2,1)}), bf16[3,1,128,2048]{2,0,1,3:T(4,128)(2,1)S(1)}, u32[]{:S(2)}, u32[]{:S(2)}) async-start(bf16[3,1,128,2048]{2,0,1,3:T(4,128)(2,1)} %copy.63), calls=%async_computation.1 | async-start | bytes 4194304 | tf_op jit(solution)/shard_map/all_to_all | solution.py:33
  26.6 233.1 %reduce-scatter.3.cloned.1.call-start = ((), (), s32[]{:S(2)}) async-start(), calls=%async_computation.9 | async-start | bytes 3932160 | tf_op jit(solution)/shard_map/reduce_scatter | solution.py:82
  169.7 4.8 %copy-start = (bf16[4,576,128]{2,1,0:T(8,128)(2,1)S(1)}, bf16[4,576,128]{2,1,0:T(8,128)(2,1)}, u32[]{:S(2)}) copy-start(bf16[4,576,128]{2,1,0:T(8,128)(2,1)} %custom-call.1) | copy-start | bytes 1769476
  200.5 121.6 %reduce-scatter.5.cloned.1.call-start = ((), (), s32[]{:S(2)}) async-start(), calls=%async_computation.10 | async-start | bytes 3932160 | tf_op jit(solution)/shard_map/reduce_scatter | solution.py:79
  209.9 9.4 %all-to-all-start.3 = ((bf16[3,1,64,512]{3,0,1,2:T(4,128)(2,1)}), bf16[3,1,64,512]{3,0,1,2:T(4,128)(2,1)S(1)}, u32[]{:S(2)}, u32[]{:S(2)}) async-start(bf16[3,1,64,512]{3,0,1,2:T(4,128)(2,1)} %copy.75), calls=%async_computation.3 | async-start | bytes 524288 | tf_op jit(solution)/shard_map/all_to_all | solution.py:73
  219.3 29.3 %all-to-all-start.2 = ((bf16[3,1,512,512]{3,0,1,2:T(4,128)(2,1)}), bf16[3,1,512,512]{3,0,1,2:T(4,128)(2,1)S(1)}, u32[]{:S(2)}, u32[]{:S(2)}) async-start(bf16[3,1,512,512]{3,0,1,2:T(4,128)(2,1)} %copy.72), calls=%async_computation.2 | async-start | bytes 4194304 | tf_op jit(solution)/shard_map/all_to_all | solution.py:74
Sparse Core Ops, SparseCore 0:
  9.6 66.1 all-gather.3
  77.3 27.2 all-gather.5
  106.2 63.4 all-gather.7
  200.7 58.9 reduce-scatter.2
  261.8 60.2 reduce-scatter.4
where the time goes:
time: 332 us; the launch traced here: 331 us
  waiting for transfers between devices  197 us (59%)
  local copies, waits for them, and re-layouts  35.1 us (11%)
  matrix products  33 us (10%)
  blocking collectives  28.5 us (9%)
  starting transfers between devices  15.2 us (5%)
  between operations  14.1 us (4%)
  other arithmetic  8.45 us (3%)
    all_gather x1, waiting for transfers between devices, local(): lax.all_gather(out_w_img, 'shard', axis=1, tiled=True)  65.1 us
    reduce_scatter x1, waiting for transfers between devices, local(): lax.psum_scatter(part_txt.astype(jnp.bfloat16), 'shard', scatter_dimensio...  60.1 us
    all_gather x1, blocking collectives, local(): lax.all_gather(grad_txt, 'seq', axis=1, tiled=True)  28.5 us
    all_gather x1, waiting for transfers between devices, local(): lax.all_gather(grad_img, 'seq', axis=1, tiled=True)  25.8 us
    all_to_all x1, waiting for transfers between devices, local(): lax.all_to_all(back_img, 'seq', split_axis=2, concat_axis=3, tiled=True)  24.9 us
    unnamed x13, local copies, waits for them, and re-layouts  12.9 us
    all_gather x1, waiting for transfers between devices, local(): lax.all_gather(out_w_txt, 'shard', axis=1, tiled=True)  8.22 us
  transfers between devices with their start and end apart: 9, of which 8 were waited for; matrix products, arithmetic and copies ran while one was open for 13% of the time, Pallas kernels for 0%

commit v1 on v0

--- a/solution.py
+++ b/solution.py
@@ -27,7 +27,7 @@
     return (output.astype(jnp.bfloat16), dquery, dkeys, dvalues)
 
 
-def local(qkv_img, qkv_txt, grad_img, grad_txt, out_w_img, out_w_txt):
+def gather_weights(qkv_img, qkv_txt, grad_img, grad_txt, out_w_img, out_w_txt):
     heads_txt, heads_img = (
         lax.all_to_all(qkv_txt, "seq", split_axis=3, concat_axis=2, tiled=True),
         lax.all_to_all(qkv_img, "seq", split_axis=3, concat_axis=2, tiled=True),
@@ -86,6 +86,62 @@
     return (ret_img, ret_txt, sum_img, sum_txt)
 
 
+def gather_tokens(qkv_img, qkv_txt, grad_img, grad_txt, out_w_img, out_w_txt):
+    text = qkv_txt.shape[2]
+    tokens = text + qkv_img.shape[2]
+    seq = lax.axis_size("seq")
+    shard = lax.axis_size("shard")
+    grad = jnp.concatenate([grad_txt[0], grad_img[0]], axis=0)
+    cols = grad.shape[1] // shard
+    grad = lax.all_to_all(
+        grad.reshape(tokens, shard, cols).transpose(1, 0, 2), "shard", 0, 0, tiled=True
+    )
+    joint = jnp.concatenate([qkv_txt[:, 0], qkv_img[:, 0]], axis=1)
+    joint = lax.all_to_all(joint, "seq", split_axis=2, concat_axis=1, tiled=True)
+    grad = lax.all_gather(grad, "seq", axis=1, tiled=False)
+    cot_txt = grad[:, :, :text]
+    cot_img = grad[:, :, text:]
+    part = jnp.concatenate(
+        [
+            jnp.einsum("bstd,hd->bsth", cot_txt, out_w_txt, preferred_element_type=jnp.float32),
+            jnp.einsum("bstd,hd->bsth", cot_img, out_w_img, preferred_element_type=jnp.float32),
+        ],
+        axis=2,
+    ).astype(jnp.bfloat16)
+    part = lax.all_to_all(part, "shard", 0, 0, tiled=True)
+    width = joint.shape[2]
+    heads = width // HEAD_DIM
+    total = seq * tokens
+    dout = jnp.sum(part.astype(jnp.float32), axis=0).astype(jnp.bfloat16).reshape(total, width)
+
+    results = []
+    for h in range(heads):
+        c = slice(h * HEAD_DIM, (h + 1) * HEAD_DIM)
+        results.append(head_backward(joint[0, :, c], joint[1, :, c], joint[2, :, c], dout[:, c]))
+    output = jnp.concatenate([r[0] for r in results], axis=1)
+    every = lax.all_gather(output, "shard", axis=0, tiled=False)
+    grads = jnp.stack([jnp.concatenate([r[i] for r in results], axis=1) for i in (1, 2, 3)])
+    back = lax.all_to_all(grads, "seq", split_axis=1, concat_axis=2, tiled=True)
+    every = every.reshape(shard, seq, tokens, width)
+    dw_txt = jnp.einsum(
+        "bsth,bstd->hd", every[:, :, :text], cot_txt, preferred_element_type=jnp.float32
+    )
+    dw_img = jnp.einsum(
+        "bsth,bstd->hd", every[:, :, text:], cot_img, preferred_element_type=jnp.float32
+    )
+    return back[:, None, text:], back[:, None, :text], dw_img, dw_txt
+
+
+def local(qkv_img, qkv_txt, grad_img, grad_txt, out_w_img, out_w_txt):
+    shard = lax.axis_size("shard")
+    weight_rows = 2 * out_w_img.shape[1]
+    token_rows = lax.axis_size("seq") * (qkv_img.shape[2] + qkv_txt.shape[2])
+    args = (qkv_img, qkv_txt, grad_img, grad_txt, out_w_img, out_w_txt)
+    if token_rows <= weight_rows:
+        return gather_tokens(*args)
+    return gather_weights(*args)
+
+
 def solution(mesh):
     return jax.shard_map(
         local,

time: 332 us -> 247 us (0.74)
  waiting for transfers between devices: 197 us -> 49.8 us
  blocking collectives: 28.5 us -> 94.1 us
  starting transfers between devices: 15.2 us -> 4.77 us
  local copies, waits for them, and re-layouts: 35.1 us -> 41.7 us
    all_gather x3 -> x2, waiting for transfers between devices: 99.1 us -> 3.32 us  [the longest x1 3.31 us: gather_tokens(): every = lax.all_gather(output, 'shard', axis=0, tiled=False)]
    all_to_all x0 -> x3, blocking collectives: none -> 94.1 us  [the longest x1 34.5 us: gather_tokens(): lax.all_to_all(joint, 'seq', split_axis=2, concat_axis=1, tiled=True)]
    reduce_scatter x2 -> x0, waiting for transfers between devices: 66.1 us -> none  [the longest x1 60.1 us: local(): lax.psum_scatter(part_txt.astype(jnp.bfloat16), 'shard', scatter_dimensio...]
    all_gather x1 -> x0, blocking collectives: 28.5 us -> none  [local(): lax.all_gather(grad_txt, 'seq', axis=1, tiled=True)]
    all_to_all x4 -> x1, waiting for transfers between devices: 29.2 us -> 46.5 us  [gather_tokens(): part = lax.all_to_all(part, 'shard', 0, 0, tiled=True)]
    all_to_all x4 -> x1, starting transfers between devices: 14.8 us -> 4.6 us  [gather_tokens(): part = lax.all_to_all(part, 'shard', 0, 0, tiled=True)]
    concatenate x0 -> x5, local copies, waits for them, and re-layouts: none -> 7.82 us  [the longest x1 4.73 us: gather_tokens(): joint = jnp.concatenate([qkv_txt[:, 0], qkv_img[:, 0]], axis=1)]
    dot_general x4, matrix products: 15.7 us -> 10.9 us  [the longest x1 3.72 us: gather_tokens(): jnp.einsum('bstd,hd->bsth', cot_img, out_w_img, preferred_element_type=jn...]
  transfers between devices with their start and end apart: 9 -> 3, of which waited for: 8 -> 2; matrix products, arithmetic and copies ran while one was open for 13% -> 18% of each run, Pallas kernels for 0% -> 0%
where the time goes in v1:
time: 247 us; the launch traced here: 246 us
  blocking collectives  94.1 us (38%)
  waiting for transfers between devices  49.8 us (20%)
  local copies, waits for them, and re-layouts  41.7 us (17%)
  matrix products  31.4 us (13%)
  between operations  14.5 us (6%)
  other arithmetic  9.4 us (4%)
  starting transfers between devices  4.77 us (2%)
    all_to_all x1, waiting for transfers between devices, gather_tokens(): part = lax.all_to_all(part, 'shard', 0, 0, tiled=True)  46.5 us
    all_to_all x1, blocking collectives, gather_tokens(): lax.all_to_all(joint, 'seq', split_axis=2, concat_axis=1, tiled=True)  34.5 us
    all_to_all x1, blocking collectives, gather_tokens(): back = lax.all_to_all(grads, 'seq', split_axis=1, concat_axis=2, tiled=True)  31 us
    all_to_all x1, blocking collectives, gather_tokens(): lax.all_to_all(grad.reshape(tokens, shard, cols).transpose(1, 0, 2), 'sha...  28.6 us
    unnamed x52, local copies, waits for them, and re-layouts  16.6 us
    all_to_all x1, local copies, waits for them, and re-layouts, gather_tokens(): lax.all_to_all(joint, 'seq', split_axis=2, concat_axis=1, tiled=True)  6.92 us
    all_to_all x2, local copies, waits for them, and re-layouts, gather_tokens(): back = lax.all_to_all(grads, 'seq', split_axis=1, concat_axis=2, tiled=True)  6.65 us
    dot_general x4, matrix products, head_backward(): jnp.dot(probs_low.T, dout, preferred_element_type=jnp.float32)  5.75 us
  transfers between devices with their start and end apart: 3, of which 2 were waited for; matrix products, arithmetic and copies ran while one was open for 18% of the time, Pallas kernels for 0%

profile of v1, /device:TPU:0, one launch (start us, length us, event | category | flops | bytes accessed | tf_op | source)
XLA Modules:
  0.0 245.7 jit_solution(16846398388405673196)
XLA Ops:
  8.3 2.0 concatenate.29
  10.4 28.6 %all_to_all.46 = bf16[4,144,768]{2,1,0:T(8,128)(2,1)} all-to-all(bf16[4,144,768]{2,1,0:T(8,128)(2,1)S(1)} %maximum_bitcast_fusion), channel_id=1, replica_groups=mesh['groups'=2,'seq'=4,'shard'=4] {'shard'}, dimensions={0} | all-to-all | bytes 1769472 | tf_op jit(solution)/shard_map/all_to_all | solution.py:96
  39.0 1.5 pad_maximum_fusion.1
  40.6 4.7 %copy.48 = bf16[3,144,2048]{1,0,2:T(4,128)(2,1)} copy(bf16[3,144,2048]{2,1,0:T(8,128)(2,1)S(1)} %pad_maximum_fusion.1) | data formatting | bytes 3538944 | tf_op jit(solution)/shard_map/concatenate | solution.py:99
  45.3 6.7 %reshape.40 = bf16[4,2,110592]{2,1,0:T(2,128)(2,1)S(1)} reshape(bf16[2048,3,144]{2,1,0:T(4,128)(2,1)} %bitcast.127) | data formatting | bytes 3538944
  52.0 34.5 %all_to_all.47 = bf16[4,2,110592]{2,1,0:T(2,128)(2,1)} all-to-all(bf16[4,2,110592]{2,1,0:T(2,128)(2,1)S(1)} %reshape.40), channel_id=1, replica_groups=mesh['groups'=2,'seq'=4,'shard'=4] {'seq'}, dimensions={0} | all-to-all | bytes 3538944 | tf_op jit(solution)/shard_map/all_to_all | solution.py:100
  86.5 7.3 %reshape.41 = bf16[2048,3,144]{2,1,0:T(4,128)(2,1)} reshape(bf16[4,2,110592]{2,1,0:T(2,128)(2,1)} %all_to_all.47) | data formatting | bytes 3538944
  93.8 6.9 %copy.50 = bf16[3,4,144,512]{3,2,1,0:T(8,128)(2,1)} copy(bf16[3,4,144,512]{2,0,3,1:T(4,128)(2,1)} %bitcast.128) | data formatting | bytes 3538944 | tf_op jit(solution)/shard_map/all_to_all | solution.py:100
  100.7 1.4 convolution_convert_fusion
  102.1 3.7 %fusion.5 = bf16[4,4,128,512]{3,2,1,0:T(8,128)(2,1)S(1)} fusion(bf16[4,4,144,768]{3,2,1,0:T(8,128)(2,1)} %bitcast.162, bf16[512,768]{1,0:T(8,128)(2,1)S(1)} %copy-done), kind=kOutput, calls=%fused_computation.6 | convolution fusion | flops 1611661312 | bytes 6029312 | tf_op jit(solution)/shard_map/bstd,hd->bsth/dot_general | solution.py:107
  105.8 1.6 pad_maximum_fusion
  107.4 4.6 %all-to-all-start.2 = ((bf16[4,4,144,512]{3,2,1,0:T(8,128)(2,1)}), bf16[4,4,144,512]{3,2,1,0:T(8,128)(2,1)}, u32[]{:S(2)}, u32[]{:S(2)}) async-start(bf16[4,4,144,512]{3,2,1,0:T(8,128)(2,1)} %pad_maximum_fusion), calls=%async_computation.2 | async-start | bytes 4718592 | tf_op jit(solution)/shard_map/all_to_all | solution.py:111
  112.2 1.5 fusion.50
  116.7 1.1 fusion.40
  118.0 1.1 fusion.39
  119.4 46.5 %all-to-all-done.2 = bf16[4,4,144,512]{3,2,1,0:T(8,128)(2,1)} async-done(((bf16[4,4,144,512]{3,2,1,0:T(8,128)(2,1)}), bf16[4,4,144,512]{3,2,1,0:T(8,128)(2,1)}, u32[]{:S(2)}, u32[]{:S(2)}) %all-to-all-start.2) | async-done | bytes 2359328 | tf_op jit(solution)/shard_map/all_to_all | solution.py:111
  165.9 3.0 %reduce_sum.85 = bf16[4,144,512]{2,1,0:T(8,128)(2,1)} reduce(bf16[4,4,144,512]{3,2,1,0:T(8,128)(2,1)} %all-to-all-done.2, bf16[]{:T(256)} %constant.8.clone.1), dimensions={0}, to_apply=%region_2.0 | reduce | flops 884736 | bytes 2949122 | tf_op jit(solution)/shard_map/reduce_sum | solution.py:115
  168.9 1.4 convolution_convert_fusion.1
  170.3 2.3 convolution_convert_fusion.2
  172.6 1.1 convolution_convert_fusion.3
  181.2 1.1 fusion.23
  183.3 1.4 multiply_convert_fusion
  184.7 1.3 fusion.28
  186.0 1.3 fusion.24
  187.7 1.7 copy.57
  189.5 31.0 %all_to_all.48 = bf16[3,576,512]{2,0,1:T(4,128)(2,1)S(1)} all-to-all(bf16[3,576,512]{2,0,1:T(4,128)(2,1)S(1)} %copy.57), channel_id=1, replica_groups=mesh['groups'=2,'seq'=4,'shard'=4] {'seq'}, dimensions={1} | all-to-all | bytes 3538944 | tf_op jit(solution)/shard_map/all_to_all | solution.py:124
  220.4 2.9 %copy.58 = bf16[3,144,4,512]{3,2,1,0:T(4,128)(2,1)} copy(bf16[3,144,4,512]{3,0,1,2:T(4,128)(2,1)S(1)} %bitcast.129) | data formatting | bytes 3538944 | tf_op jit(solution)/shard_map/all_to_all | solution.py:124
  223.3 3.7 %all_to_all.41 = bf16[3,144,2048]{2,1,0:T(8,128)(2,1)S(1)} reshape(bf16[3,144,4,512]{3,2,1,0:T(4,128)(2,1)} %copy.58) | data formatting | bytes 3538944 | tf_op jit(solution)/shard_map/all_to_all | solution.py:124
  227.8 1.2 slice_bitcast_fusion
  229.0 3.3 %all-gather.7.cloned.1.call-done = bf16[2304,512]{1,0:T(8,128)(2,1)} async-done(((bf16[576,512]{1,0:T(8,128)(2,1)}), bf16[2304,512]{1,0:T(8,128)(2,1)}) %all-gather.7.cloned.1.call-update) | async-done | bytes 2359312 | tf_op jit(solution)/shard_map/all_gather | solution.py:122
  232.4 2.8 %convolution_bitcast_fusion = f32[512,768]{1,0:T(8,128)} fusion(bf16[4,4,144,768]{3,2,1,0:T(8,128)(2,1)} %bitcast.163, bf16[4,4,144,512]{3,2,1,0:T(8,128)(2,1)} %bitcast.165), kind=kOutput, calls=%fused_computation.11 | convolution fusion | flops 201326592 | bytes 2228224 | tf_op jit(solution)/shard_map/bsth,bstd->hd/dot_general | solution.py:126
  235.9 3.0 %fusion.8 = f32[512,768]{1,0:T(8,128)} fusion(bf16[4,4,144,768]{3,2,1,0:T(8,128)(2,1)S(1)} %bitcast.164, bf16[4,4,144,512]{3,2,1,0:T(8,128)(2,1)S(1)} %bitcast.166), kind=kOutput, calls=%fused_computation.10 | convolution fusion | flops 1610612736 | bytes 6815744 | tf_op jit(solution)/shard_map/bsth,bstd->hd/dot_general | solution.py:129
  (86 shorter events, 15.0 us)
Async XLA Ops:
  7.2 94.9 %copy-start = (bf16[512,768]{1,0:T(8,128)(2,1)S(1)}, bf16[512,768]{1,0:T(8,128)(2,1)}, u32[]{:S(2)}) copy-start(bf16[512,768]{1,0:T(8,128)(2,1)} %param.10) | copy-start | bytes 2359300
  7.2 93.5 %all-gather.5.cloned.1.call-start = ((), (), s32[]{:S(2)}) async-start(), calls=%async_computation.4 | async-start | bytes 4423680 | tf_op jit(solution)/shard_map/all_gather | solution.py:101
  10.4 28.6 %copy-start.19 = (bf16[3,1,16,2048]{3,2,1,0:T(8,128)(2,1)S(1)}, bf16[3,1,16,2048]{3,2,1,0:T(8,128)(2,1)}, u32[]{:S(2)}) copy-start(bf16[3,1,16,2048]{3,2,1,0:T(8,128)(2,1)} %param.7) | copy-start | bytes 589828
  93.8 6.9 %copy-start.24 = (bf16[512,768]{1,0:T(8,128)(2,1)S(1)}, bf16[512,768]{1,0:T(8,128)(2,1)}, u32[]{:S(2)}) copy-start(bf16[512,768]{1,0:T(8,128)(2,1)} %param.11) | copy-start | bytes 2359300
  107.4 58.5 %all-to-all-start.2 = ((bf16[4,4,144,512]{3,2,1,0:T(8,128)(2,1)}), bf16[4,4,144,512]{3,2,1,0:T(8,128)(2,1)}, u32[]{:S(2)}, u32[]{:S(2)}) async-start(bf16[4,4,144,512]{3,2,1,0:T(8,128)(2,1)} %pad_maximum_fusion), calls=%async_computation.2 | async-start | bytes 4718592 | tf_op jit(solution)/shard_map/all_to_all | solution.py:111
  112.0 120.3 %all-gather.7.cloned.1.call-start = ((), (), s32[]{:S(2)}) async-start(), calls=%async_computation.5 | async-start | bytes 2949120 | tf_op jit(solution)/shard_map/all_gather | solution.py:122
  112.1 1.7 copy-start.8
  114.3 2.1 copy-start.2
  114.9 2.9 %copy-start.4 = (f32[576,576]{0,1:T(8,128)}, f32[576,576]{0,1:T(8,128)S(1)}, u32[]{:S(2)}) copy-start(f32[576,576]{0,1:T(8,128)S(1)} %get-tuple-element.17) | copy-start | bytes 3981316
  115.5 3.6 %copy-start.6 = (f32[576,576]{0,1:T(8,128)}, f32[576,576]{0,1:T(8,128)S(1)}, u32[]{:S(2)}) copy-start(f32[576,576]{0,1:T(8,128)S(1)} %get-tuple-element.19) | copy-start | bytes 3981316
  116.6 1.4 copy-start.10
  118.0 1.1 copy-start.11
  168.9 3.7 %copy-start.12 = (bf16[576,576]{0,1:T(8,128)(2,1)S(1)}, bf16[576,576]{0,1:T(8,128)(2,1)}, u32[]{:S(2)}) copy-start(bf16[576,576]{0,1:T(8,128)(2,1)} %copy-done.11) | copy-start | bytes 1990660
  168.9 3.7 %copy-start.13 = (bf16[4,144,512]{2,1,0:T(8,128)(2,1)S(1)}, bf16[4,144,512]{2,1,0:T(8,128)(2,1)}, u32[]{:S(2)}) copy-start(bf16[4,144,512]{2,1,0:T(8,128)(2,1)} %reduce_sum.85) | copy-start | bytes 1769476
  170.3 4.4 %copy-start.9 = (bf16[3,4,144,512]{3,2,1,0:T(8,128)(2,1)S(1)}, bf16[3,4,144,512]{3,2,1,0:T(8,128)(2,1)}, u32[]{:S(2)}) copy-start(bf16[3,4,144,512]{3,2,1,0:T(8,128)(2,1)} %copy.50) | copy-start | bytes 5308420
  170.3 4.4 %copy-start.14 = (f32[576,128]{1,0:T(8,128)S(1)}, f32[576,128]{1,0:T(8,128)}, u32[]{:S(2)}) copy-start(f32[576,128]{1,0:T(8,128)} %fusion.40) | copy-start | bytes 884740
  170.3 4.4 %copy-start.15 = (f32[576,128]{1,0:T(8,128)S(1)}, f32[576,128]{1,0:T(8,128)}, u32[]{:S(2)}) copy-start(f32[576,128]{1,0:T(8,128)} %fusion.39) | copy-start | bytes 884740
  174.7 1.4 copy-start.7
  176.6 1.4 copy-start.5
  178.4 1.4 copy-start.3
  181.2 2.0 copy-start.16
  181.2 2.0 copy-start.17
  181.2 2.0 copy-start.18
  184.7 2.7 %copy-start.20 = (bf16[576,128]{1,0:T(8,128)(2,1)S(1)}, bf16[576,128]{1,0:T(8,128)(2,1)}, u32[]{:S(2)}) copy-start(bf16[576,128]{1,0:T(8,128)(2,1)} %fusion.27) | copy-start | bytes 442372
  184.7 2.7 %copy-start.21 = (bf16[576,128]{1,0:T(8,128)(2,1)S(1)}, bf16[576,128]{1,0:T(8,128)(2,1)}, u32[]{:S(2)}) copy-start(bf16[576,128]{1,0:T(8,128)(2,1)} %fusion.23) | copy-start | bytes 442372
  232.3 2.8 %copy-start.22 = (bf16[4,576,768]{2,1,0:T(8,128)(2,1)S(1)}, bf16[4,576,768]{2,1,0:T(8,128)(2,1)}, u32[]{:S(2)}) copy-start(bf16[4,576,768]{2,1,0:T(8,128)(2,1)} %all-gather.5.cloned.1.call-done) | copy-start | bytes 10616836
  232.4 3.5 %copy-start.23 = (bf16[2304,512]{1,0:T(8,128)(2,1)S(1)}, bf16[2304,512]{1,0:T(8,128)(2,1)}, u32[]{:S(2)}) copy-start(bf16[2304,512]{1,0:T(8,128)(2,1)} %all-gather.7.cloned.1.call-done) | copy-start | bytes 7077892
  235.9 3.0 %copy-start.1 = (bf16[512,768]{1,0:T(8,128)(2,1)S(1)}, bf16[512,768]{1,0:T(8,128)(2,1)}, u32[]{:S(2)}) copy-start(bf16[512,768]{1,0:T(8,128)(2,1)} %param.10) | copy-start | bytes 2359300
Sparse Core Ops, SparseCore 0:
  39.1 39.0 all-gather.4
  183.3 49.0 all-gather.6

commit v2 on v1

--- a/solution.py
+++ b/solution.py
@@ -1,6 +1,10 @@
+import functools
+
 import jax
 import jax.numpy as jnp
 from jax import lax
+from jax.experimental import pallas as pl
+from jax.experimental.pallas import tpu as pltpu
 from jax.sharding import PartitionSpec as P
 
 HEAD_DIM = 128
@@ -132,11 +136,293 @@
     return back[:, None, text:], back[:, None, :text], dw_img, dw_txt
 
 
+NT = (((1,), (1,)), ((), ()))
+TN = (((0,), (0,)), ((), ()))
+
+
+def fused_kernel(
+    S, Z, text, qkv_img, qkv_txt, grad_img, grad_txt, w_img, w_txt,
+    out_img, out_txt, dw_img, dw_txt,
+    gbuf, qbuf, heads, G, psend, part, own, probs_s, o_s, every, dout_s, dbuf, rbuf,
+    local_sem, gz_s, gz_r, gx_s, gx_r, q_s, q_r, p_s, p_r, o_snd, o_r, d_s, d_r,
+):
+    T = gbuf.shape[0]
+    C = w_img.shape[1]
+    W = w_img.shape[0]
+    H = W // HEAD_DIM
+    s = lax.axis_index("seq")
+    z = lax.axis_index("shard")
+    core = s + 1 - 2 * lax.rem(s, 2)
+    cross = lax.rem(s + 2, S)
+    diag = lax.rem(core + 2, S)
+    seqs = [core, cross, diag]
+    imgs = [lax.rem(z + k, Z) for k in range(Z)]
+
+    def rows(block):
+        return pl.ds(pl.multiple_of(block * T, 16), T)
+
+    def cols(block, width):
+        return pl.ds(pl.multiple_of(block * width, 128), width)
+
+    stage = [
+        pltpu.make_async_copy(grad_txt.at[0], gbuf.at[pl.ds(0, text)], local_sem.at[0]),
+        pltpu.make_async_copy(grad_img.at[0], gbuf.at[pl.ds(text, T - text)], local_sem.at[1]),
+        pltpu.make_async_copy(qkv_txt.at[:, 0], qbuf.at[:, pl.ds(0, text)], local_sem.at[2]),
+        pltpu.make_async_copy(
+            qkv_img.at[:, 0], qbuf.at[:, pl.ds(text, T - text)], local_sem.at[3]
+        ),
+    ]
+    for c in stage:
+        c.start()
+    barrier = pltpu.get_barrier_semaphore()
+    for t in seqs:
+        pl.semaphore_signal(
+            barrier, inc=1, device_id={"seq": t}, device_id_type=pl.DeviceIdType.MESH
+        )
+    for t in imgs[1:]:
+        pl.semaphore_signal(
+            barrier, inc=1, device_id={"shard": t}, device_id_type=pl.DeviceIdType.MESH
+        )
+    pl.semaphore_wait(barrier, S + Z - 2)
+
+    def remote(src, dst, send, recv, where):
+        return pltpu.make_async_remote_copy(
+            src_ref=src, dst_ref=dst, send_sem=send, recv_sem=recv,
+            device_id=where, device_id_type=pl.DeviceIdType.MESH,
+        )
+
+    sends = []
+
+    def start(*args):
+        c = remote(*args)
+        c.start()
+        sends.append(c)
+
+    def block(i, t):
+        return G.at[i, rows(t)]
+
+    def gx_start(i, t, kind, where):
+        start(block(i, t), block(i, t), gx_s.at[i, kind], gx_r.at[i, kind], {"seq": where})
+
+    def gx_wait(i, t, kind):
+        remote(
+            block(i, t), block(i, t), gx_s.at[i, kind], gx_r.at[i, kind], {"seq": core}
+        ).wait_recv()
+
+    stage[0].wait()
+    stage[1].wait()
+    for k in range(1, Z):
+        i = imgs[k]
+        start(gbuf.at[:, cols(i, C)], block(z, s), gz_s.at[k], gz_r.at[z], {"shard": i})
+    mine = pltpu.make_async_copy(gbuf.at[:, cols(z, C)], block(z, s), local_sem.at[4])
+    mine.start()
+    mine.wait()
+    gx_start(z, s, 0, cross)
+    gx_start(z, s, 1, core)
+    stage[2].wait()
+    stage[3].wait()
+    for n, t in enumerate((cross, diag, core)):
+        start(qbuf.at[:, :, cols(t, W)], heads.at[:, rows(s)], q_s.at[n], q_r.at[s], {"seq": t})
+    mine_q = pltpu.make_async_copy(qbuf.at[:, :, cols(s, W)], heads.at[:, rows(s)], local_sem.at[5])
+    mine_q.start()
+
+    def split(ref, i):
+        image = jnp.concatenate([ref[i, t * T + text:(t + 1) * T, :] for t in range(S)], axis=0)
+        words = jnp.concatenate([ref[i, t * T:t * T + text, :] for t in range(S)], axis=0)
+        return image, words
+
+    def partial(i, store):
+        image, words = split(G, i)
+        pi = lax.dot_general(image, w_img[...], NT, preferred_element_type=jnp.float32)
+        pt = lax.dot_general(words, w_txt[...], NT, preferred_element_type=jnp.float32)
+        n = T - text
+        for t in range(S):
+            store(t * T, text, pt[t * text:(t + 1) * text])
+            store(t * T + text, n, pi[t * n:(t + 1) * n])
+
+    def relay(k):
+        gx_wait(imgs[k], cross, 0)
+        gx_start(imgs[k], cross, 2, core)
+
+    def produce(k):
+        i = imgs[k]
+        gx_wait(i, core, 1)
+        gx_wait(i, diag, 2)
+
+        def store(r, n, v):
+            psend[k - 1, r:r + n, :] = v.astype(jnp.bfloat16)
+
+        partial(i, store)
+        start(psend.at[k - 1], part.at[z], p_s.at[k], p_r.at[z], {"shard": i})
+
+    for k in range(1, Z):
+        i = imgs[k]
+        remote(block(i, s), block(i, s), gz_s.at[k], gz_r.at[i], {"shard": i}).wait_recv()
+        gx_start(i, s, 0, cross)
+        gx_start(i, s, 1, core)
+        relay(k - 1)
+        if k >= 3:
+            produce(k - 2)
+    relay(Z - 1)
+    for k in range(max(1, Z - 2), Z):
+        produce(k)
+    gx_wait(z, core, 1)
+    gx_wait(z, diag, 2)
+
+    def store_own(r, n, v):
+        own[r:r + n, :] = v
+
+    partial(z, store_own)
+
+    mine_q.wait()
+    for t in seqs:
+        remote(
+            heads.at[:, rows(t)], heads.at[:, rows(t)], q_s.at[0], q_r.at[t], {"seq": t}
+        ).wait_recv()
+    scale = HEAD_DIM ** (-0.5)
+
+    def forward(h, carry):
+        c = cols(h, HEAD_DIM)
+        scores = lax.dot_general(
+            heads[0, :, c], heads[1, :, c], NT, preferred_element_type=jnp.float32
+        ) * scale
+        expo = jnp.exp(scores - jnp.max(scores, axis=-1, keepdims=True))
+        probs = expo * (1.0 / jnp.sum(expo, axis=-1, keepdims=True))
+        probs_s[h] = probs
+        o = jnp.dot(probs.astype(jnp.bfloat16), heads[2, :, c], preferred_element_type=jnp.float32)
+        o_s[:, c] = o
+        every[z, :, c] = o.astype(jnp.bfloat16)
+        return carry
+
+    lax.fori_loop(0, H, forward, 0)
+    for k in range(1, Z):
+        start(every.at[z], every.at[z], o_snd.at[k], o_r.at[z], {"shard": imgs[k]})
+
+    for k in range(1, Z):
+        i = imgs[k]
+        remote(part.at[i], part.at[i], p_s.at[k], p_r.at[i], {"shard": i}).wait_recv()
+    total = own[...]
+    for k in range(1, Z):
+        total = total + part[imgs[k]].astype(jnp.float32)
+    dout_s[...] = total.astype(jnp.bfloat16)
+
+    def d_copy(h, n, t):
+        return remote(
+            dbuf.at[:, rows(t), cols(h, HEAD_DIM)],
+            rbuf.at[:, :, cols(s * H + h, HEAD_DIM)],
+            d_s.at[h, n], d_r.at[h, n], {"seq": t},
+        )
+
+    def backward(h, carry):
+        c = cols(h, HEAD_DIM)
+        dout = dout_s[:, c]
+        probs = probs_s[h]
+        dprobs = lax.dot_general(dout, heads[2, :, c], NT, preferred_element_type=jnp.float32)
+        delta = jnp.sum(dout.astype(jnp.float32) * o_s[:, c], axis=-1, keepdims=True)
+        ds = (probs * (dprobs - delta)).astype(jnp.bfloat16)
+        dq = jnp.dot(ds, heads[1, :, c], preferred_element_type=jnp.float32) * scale
+        dk = lax.dot_general(ds, heads[0, :, c], TN, preferred_element_type=jnp.float32) * scale
+        dv = lax.dot_general(
+            probs.astype(jnp.bfloat16), dout, TN, preferred_element_type=jnp.float32
+        )
+        dbuf[0, :, c] = dq.astype(jnp.bfloat16)
+        dbuf[1, :, c] = dk.astype(jnp.bfloat16)
+        dbuf[2, :, c] = dv.astype(jnp.bfloat16)
+        for n, t in ((1, cross), (2, diag), (0, core)):
+            d_copy(h, n, t).start()
+        return carry
+
+    lax.fori_loop(0, H, backward, 0)
+    mine_d = pltpu.make_async_copy(dbuf.at[:, rows(s)], rbuf.at[:, :, cols(s, W)], local_sem.at[6])
+    mine_d.start()
+
+    for k in range(Z):
+        i = imgs[k]
+        if k:
+            remote(every.at[i], every.at[i], o_snd.at[k], o_r.at[i], {"shard": i}).wait_recv()
+        ob_i, ob_t = split(every, i)
+        g_i, g_t = split(G, i)
+        di = lax.dot_general(ob_i, g_i, TN, preferred_element_type=jnp.float32)
+        dt = lax.dot_general(ob_t, g_t, TN, preferred_element_type=jnp.float32)
+        if k:
+            dw_img[...] += di
+            dw_txt[...] += dt
+        else:
+            dw_img[...] = di
+            dw_txt[...] = dt
+
+    mine_d.wait()
+    for h in range(H):
+        for n, t in enumerate(seqs):
+            d_copy(h, n, t).wait_send()
+            remote(
+                rbuf.at[:, :, cols(t * H + h, HEAD_DIM)],
+                rbuf.at[:, :, cols(t * H + h, HEAD_DIM)],
+                d_s.at[h, n], d_r.at[h, n], {"seq": t},
+            ).wait_recv()
+    last = [
+        pltpu.make_async_copy(rbuf.at[:, pl.ds(0, text)], out_txt.at[:, 0], local_sem.at[0]),
+        pltpu.make_async_copy(rbuf.at[:, pl.ds(text, T - text)], out_img.at[:, 0], local_sem.at[1]),
+    ]
+    for c in last:
+        c.start()
+    for c in sends:
+        c.wait_send()
+    for c in last:
+        c.wait()
+
+
+def fused(qkv_img, qkv_txt, grad_img, grad_txt, out_w_img, out_w_txt):
+    S = lax.axis_size("seq")
+    Z = lax.axis_size("shard")
+    text = qkv_txt.shape[2]
+    T = text + qkv_img.shape[2]
+    HDW = qkv_img.shape[3]
+    width = grad_img.shape[2]
+    W, C = out_w_img.shape
+    H = W // HEAD_DIM
+    N = S * T
+    bf, f4 = jnp.bfloat16, jnp.float32
+    V, D = pltpu.VMEM, pltpu.SemaphoreType.DMA
+    hbm = pl.BlockSpec(memory_space=pl.ANY)
+    vm = pl.BlockSpec(memory_space=pltpu.VMEM)
+    return pl.pallas_call(
+        functools.partial(fused_kernel, S, Z, text),
+        out_shape=(
+            jax.ShapeDtypeStruct(qkv_img.shape, bf),
+            jax.ShapeDtypeStruct(qkv_txt.shape, bf),
+            jax.ShapeDtypeStruct((W, C), f4),
+            jax.ShapeDtypeStruct((W, C), f4),
+        ),
+        in_specs=[hbm, hbm, hbm, hbm, vm, vm],
+        out_specs=(hbm, hbm, vm, vm),
+        scratch_shapes=[
+            V((T, width), bf), V((3, T, HDW), bf), V((3, N, W), bf), V((Z, N, C), bf),
+            V((Z - 1, N, W), bf), V((Z, N, W), bf), V((N, W), f4), V((H, N, N), f4),
+            V((N, W), f4), V((Z, N, W), bf), V((N, W), bf), V((3, N, W), bf), V((3, T, HDW), bf),
+            D((7,)), D((Z,)), D((Z,)), D((Z, 3)), D((Z, 3)), D((S,)), D((S,)),
+            D((Z,)), D((Z,)), D((Z,)), D((Z,)), D((H, 3)), D((H, 3)),
+        ],
+        compiler_params=pltpu.CompilerParams(
+            collective_id=0, has_side_effects=True, vmem_limit_bytes=52 * 1024 * 1024
+        ),
+    )(qkv_img, qkv_txt, grad_img, grad_txt, out_w_img, out_w_txt)
+
+
 def local(qkv_img, qkv_txt, grad_img, grad_txt, out_w_img, out_w_txt):
     shard = lax.axis_size("shard")
     weight_rows = 2 * out_w_img.shape[1]
     token_rows = lax.axis_size("seq") * (qkv_img.shape[2] + qkv_txt.shape[2])
     args = (qkv_img, qkv_txt, grad_img, grad_txt, out_w_img, out_w_txt)
+    if (
+        token_rows <= weight_rows
+        and lax.axis_size("seq") == 4
+        and lax.axis_size("shard") == 4
+        and out_w_img.shape[1] % 128 == 0
+        and qkv_txt.shape[2] % 16 == 0
+        and qkv_img.shape[2] % 16 == 0
+    ):
+        return fused(*args)
     if token_rows <= weight_rows:
         return gather_tokens(*args)
     return gather_weights(*args)

time: 247 us -> 160 us (0.65)
  the two profiles are of different devices: /device:TPU:0 before, /device:TPU:11 now
where the time goes in v2:
time: 160 us
  Pallas kernels  149 us (93%)
  local copies, waits for them, and re-layouts  9.59 us (6%)
    pallas_call x1, Pallas kernels, fused(): pl.pallas_call(functools.partial(fused_kernel, S, Z, text), out_shape=(ja...  149 us
    unnamed x14, local copies, waits for them, and re-layouts  9.59 us

profile of v2, /device:TPU:11, one launch (start us, length us, event | category | flops | bytes accessed | tf_op | source)
XLA Modules:
  0.0 159.6 jit_solution(2488389143625609351)
XLA Ops:
  0.6 0.0 copy-start
  0.6 1.1 copy-done
  1.8 0.0 copy-start.1
  1.8 0.9 copy-done.1
  2.7 0.0 copy-start.2
  2.7 0.9 copy-done.2
  3.6 149.3 %shard_map.93 = (bf16[3,1,128,2048]{3,2,1,0:T(8,128)(2,1)}, bf16[3,1,16,2048]{3,2,1,0:T(8,128)(2,1)S(1)}, f32[512,768]{1,0:T(8,128)}, f32[512,768]{1,0:T(8,128)}) custom-call(bf16[3,1,128,2048]{3,2,1,0:T(8,128)(2,1)} %qkv_img.1, bf16[3,1,16,2048]{3,2,1,0:T(8,128)(2,1)S(1)} %copy-done.1, bf16[1,128,3072]{2,1,0:T(8,128)(2,1)S(1)} %copy-done, ...), custom_call_target="tpu_custom_call" | custom-call | tf_op jit(solution)/shard_map/pallas_call | solution.py:389
  152.9 0.0 copy-start.4
  152.9 2.8 %copy.14 = bf16[3,1,128,2048]{3,2,1,0:T(8,128)(2,1)} copy(bf16[3,1,128,2048]{3,2,1,0:T(8,128)(2,1)} %get-tuple-element.8) | data formatting | bytes 3145728
  155.8 0.7 copy.15
  156.5 0.0 copy-done.4
  156.5 0.0 copy-start.3
  156.5 1.1 copy.16
  157.6 0.8 copy-done.3
  158.4 1.1 copy.17
Async XLA Ops:
  0.6 1.1 copy-start
  1.8 0.9 copy-start.1
  2.7 0.9 copy-start.2
  152.9 3.5 %copy-start.4 = (f32[512,768]{1,0:T(8,128)S(1)}, f32[512,768]{1,0:T(8,128)}, u32[]{:S(2)}) copy-start(f32[512,768]{1,0:T(8,128)} %get-tuple-element.10) | copy-start | bytes 4718596
  156.5 2.0 %copy-start.3 = (f32[512,768]{1,0:T(8,128)S(1)}, f32[512,768]{1,0:T(8,128)}, u32[]{:S(2)}) copy-start(f32[512,768]{1,0:T(8,128)} %get-tuple-element.11) | copy-start | bytes 4718596

commit v3 on v2

--- a/solution.py
+++ b/solution.py
@@ -143,7 +143,7 @@
 def fused_kernel(
     S, Z, text, qkv_img, qkv_txt, grad_img, grad_txt, w_img, w_txt,
     out_img, out_txt, dw_img, dw_txt,
-    gbuf, qbuf, heads, G, psend, part, own, probs_s, o_s, every, dout_s, dbuf, rbuf,
+    gbuf, qbuf, heads, G, psend, part, own, probs_s, o_s, every, dbuf, rbuf,
     local_sem, gz_s, gz_r, gx_s, gx_r, q_s, q_r, p_s, p_r, o_snd, o_r, d_s, d_r,
 ):
     T = gbuf.shape[0]
@@ -253,32 +253,7 @@
             psend[k - 1, r:r + n, :] = v.astype(jnp.bfloat16)
 
         partial(i, store)
-        start(psend.at[k - 1], part.at[z], p_s.at[k], p_r.at[z], {"shard": i})
-
-    for k in range(1, Z):
-        i = imgs[k]
-        remote(block(i, s), block(i, s), gz_s.at[k], gz_r.at[i], {"shard": i}).wait_recv()
-        gx_start(i, s, 0, cross)
-        gx_start(i, s, 1, core)
-        relay(k - 1)
-        if k >= 3:
-            produce(k - 2)
-    relay(Z - 1)
-    for k in range(max(1, Z - 2), Z):
-        produce(k)
-    gx_wait(z, core, 1)
-    gx_wait(z, diag, 2)
-
-    def store_own(r, n, v):
-        own[r:r + n, :] = v
-
-    partial(z, store_own)
-
-    mine_q.wait()
-    for t in seqs:
-        remote(
-            heads.at[:, rows(t)], heads.at[:, rows(t)], q_s.at[0], q_r.at[t], {"seq": t}
-        ).wait_recv()
+
     scale = HEAD_DIM ** (-0.5)
 
     def forward(h, carry):
@@ -294,17 +269,73 @@
         every[z, :, c] = o.astype(jnp.bfloat16)
         return carry
 
-    lax.fori_loop(0, H, forward, 0)
-    for k in range(1, Z):
-        start(every.at[z], every.at[z], o_snd.at[k], o_r.at[z], {"shard": imgs[k]})
-
     for k in range(1, Z):
         i = imgs[k]
-        remote(part.at[i], part.at[i], p_s.at[k], p_r.at[i], {"shard": i}).wait_recv()
-    total = own[...]
+        remote(block(i, s), block(i, s), gz_s.at[k], gz_r.at[i], {"shard": i}).wait_recv()
+        gx_start(i, s, 0, cross)
+        gx_start(i, s, 1, core)
+    mine_q.wait()
+    for t in seqs:
+        remote(
+            heads.at[:, rows(t)], heads.at[:, rows(t)], q_s.at[0], q_r.at[t], {"seq": t}
+        ).wait_recv()
+
+    def o_copy(j, way, to):
+        return remote(every.at[j], every.at[j], o_snd.at[j, way], o_r.at[j], {"shard": to})
+
+    def hop(distance, act):
+        left, right = z - distance, z + distance
+
+        @pl.when((left >= 0) & (z < Z - 1))
+        def _():
+            act(o_copy(left, 0, z + 1))
+
+        @pl.when((right < Z) & (z > 0))
+        def _():
+            act(o_copy(right, 1, z - 1))
+
+    def arrive(distance):
+        for j, ok in ((z - distance, z >= distance), (z + distance, z + distance < Z)):
+
+            @pl.when(ok)
+            def _():
+                remote(every.at[j], every.at[j], o_snd.at[j, 0], o_r.at[j], {"shard": imgs[1]}).wait_recv()
+
+    per = -(-H // Z)
+    for k in range(Z):
+        lax.fori_loop(min(H, k * per), min(H, (k + 1) * per), forward, 0)
+        if k < Z - 1:
+            relay(k)
+    hop(0, lambda c: c.start())
+    relay(Z - 1)
     for k in range(1, Z):
-        total = total + part[imgs[k]].astype(jnp.float32)
-    dout_s[...] = total.astype(jnp.bfloat16)
+        produce(k)
+    if Z > 2:
+        arrive(1)
+        hop(1, lambda c: c.start())
+    for h in range(H):
+        c = pl.ds(h * HEAD_DIM, HEAD_DIM)
+        for k in range(Z - 1, 0, -1):
+            start(
+                psend.at[k - 1, :, c], part.at[z, :, c],
+                p_s.at[k, h], p_r.at[z, h], {"shard": imgs[k]},
+            )
+    gx_wait(z, core, 1)
+    gx_wait(z, diag, 2)
+
+    def store_own(r, n, v):
+        own[r:r + n, :] = v
+
+    partial(z, store_own)
+
+    def weight_grad(i):
+        ob_i, ob_t = split(every, i)
+        g_i, g_t = split(G, i)
+        di = lax.dot_general(ob_i, g_i, TN, preferred_element_type=jnp.float32)
+        dt = lax.dot_general(ob_t, g_t, TN, preferred_element_type=jnp.float32)
+        return di, dt
+
+    dw_img[...], dw_txt[...] = weight_grad(z)
 
     def d_copy(h, n, t):
         return remote(
@@ -315,7 +346,14 @@
 
     def backward(h, carry):
         c = cols(h, HEAD_DIM)
-        dout = dout_s[:, c]
+        total = own[:, c]
+        for k in range(1, Z):
+            i = imgs[k]
+            remote(
+                part.at[i, :, c], part.at[i, :, c], p_s.at[k, h], p_r.at[i, h], {"shard": i}
+            ).wait_recv()
+            total = total + part[i, :, c].astype(jnp.float32)
+        dout = total.astype(jnp.bfloat16)
         probs = probs_s[h]
         dprobs = lax.dot_general(dout, heads[2, :, c], NT, preferred_element_type=jnp.float32)
         delta = jnp.sum(dout.astype(jnp.float32) * o_s[:, c], axis=-1, keepdims=True)
@@ -332,24 +370,24 @@
             d_copy(h, n, t).start()
         return carry
 
-    lax.fori_loop(0, H, backward, 0)
+    half = (H + 1) // 2
+    lax.fori_loop(0, half, backward, 0)
+    for distance in range(2, Z - 1):
+        arrive(distance)
+        hop(distance, lambda c: c.start())
+    lax.fori_loop(half, H, backward, 0)
     mine_d = pltpu.make_async_copy(dbuf.at[:, rows(s)], rbuf.at[:, :, cols(s, W)], local_sem.at[6])
     mine_d.start()
-
-    for k in range(Z):
-        i = imgs[k]
-        if k:
-            remote(every.at[i], every.at[i], o_snd.at[k], o_r.at[i], {"shard": i}).wait_recv()
-        ob_i, ob_t = split(every, i)
-        g_i, g_t = split(G, i)
-        di = lax.dot_general(ob_i, g_i, TN, preferred_element_type=jnp.float32)
-        dt = lax.dot_general(ob_t, g_t, TN, preferred_element_type=jnp.float32)
-        if k:
-            dw_img[...] += di
-            dw_txt[...] += dt
-        else:
-            dw_img[...] = di
-            dw_txt[...] = dt
+    for distance in range(max(1, Z - 1), Z):
+        arrive(distance)
+
+    def add_image(k, carry):
+        di, dt = weight_grad(lax.rem(z + k, Z))
+        dw_img[...] += di
+        dw_txt[...] += dt
+        return carry
+
+    lax.fori_loop(1, Z, add_image, 0)
 
     mine_d.wait()
     for h in range(H):
@@ -368,6 +406,8 @@
         c.start()
     for c in sends:
         c.wait_send()
+    for distance in range(Z - 1):
+        hop(distance, lambda c: c.wait_send())
     for c in last:
         c.wait()
 
@@ -399,9 +439,9 @@
         scratch_shapes=[
             V((T, width), bf), V((3, T, HDW), bf), V((3, N, W), bf), V((Z, N, C), bf),
             V((Z - 1, N, W), bf), V((Z, N, W), bf), V((N, W), f4), V((H, N, N), f4),
-            V((N, W), f4), V((Z, N, W), bf), V((N, W), bf), V((3, N, W), bf), V((3, T, HDW), bf),
+            V((N, W), f4), V((Z, N, W), bf), V((3, N, W), bf), V((3, T, HDW), bf),
             D((7,)), D((Z,)), D((Z,)), D((Z, 3)), D((Z, 3)), D((S,)), D((S,)),
-            D((Z,)), D((Z,)), D((Z,)), D((Z,)), D((H, 3)), D((H, 3)),
+            D((Z, H)), D((Z, H)), D((Z, 2)), D((Z,)), D((H, 3)), D((H, 3)),
         ],
         compiler_params=pltpu.CompilerParams(
             collective_id=0, has_side_effects=True, vmem_limit_bytes=52 * 1024 * 1024

time: 160 us -> 142 us (0.89)
  the two profiles are of different devices: /device:TPU:11 before, /device:TPU:0 now
where the time goes in v3:
time: 142 us
  Pallas kernels  132 us (93%)
  local copies, waits for them, and re-layouts  9.59 us (7%)
    pallas_call x1, Pallas kernels, fused(): pl.pallas_call(functools.partial(fused_kernel, S, Z, text), out_shape=(ja...  132 us
    unnamed x14, local copies, waits for them, and re-layouts  9.59 us

profile of v3, /device:TPU:0, one launch (start us, length us, event | category | flops | bytes accessed | tf_op | source)
XLA Modules:
  0.0 142.0 jit_solution(12921105369443608146)
XLA Ops:
  0.6 0.0 copy-start
  0.6 1.1 copy-done
  1.8 0.0 copy-start.1
  1.8 0.9 copy-done.1
  2.7 0.0 copy-start.2
  2.7 0.9 copy-done.2
  3.6 131.7 %shard_map.93 = (bf16[3,1,128,2048]{3,2,1,0:T(8,128)(2,1)}, bf16[3,1,16,2048]{3,2,1,0:T(8,128)(2,1)S(1)}, f32[512,768]{1,0:T(8,128)}, f32[512,768]{1,0:T(8,128)}) custom-call(bf16[3,1,128,2048]{3,2,1,0:T(8,128)(2,1)} %qkv_img.1, bf16[3,1,16,2048]{3,2,1,0:T(8,128)(2,1)S(1)} %copy-done.1, bf16[1,128,3072]{2,1,0:T(8,128)(2,1)S(1)} %copy-done, ...), custom_call_target="tpu_custom_call" | custom-call | tf_op jit(solution)/shard_map/pallas_call | solution.py:429
  135.3 0.0 copy-start.4
  135.3 2.8 %copy.14 = bf16[3,1,128,2048]{3,2,1,0:T(8,128)(2,1)} copy(bf16[3,1,128,2048]{3,2,1,0:T(8,128)(2,1)} %get-tuple-element.8) | data formatting | bytes 3145728
  138.2 0.7 copy.15
  138.9 0.0 copy-done.4
  138.9 0.0 copy-start.3
  138.9 1.1 copy.16
  140.0 0.8 copy-done.3
  140.8 1.1 copy.17
Async XLA Ops:
  0.6 1.1 copy-start
  1.8 0.9 copy-start.1
  2.7 0.9 copy-start.2
  135.3 3.5 %copy-start.4 = (f32[512,768]{1,0:T(8,128)S(1)}, f32[512,768]{1,0:T(8,128)}, u32[]{:S(2)}) copy-start(f32[512,768]{1,0:T(8,128)} %get-tuple-element.10) | copy-start | bytes 4718596
  138.9 2.0 %copy-start.3 = (f32[512,768]{1,0:T(8,128)S(1)}, f32[512,768]{1,0:T(8,128)}, u32[]{:S(2)}) copy-start(f32[512,768]{1,0:T(8,128)} %get-tuple-element.11) | copy-start | bytes 4718596

commit v4 on v3

--- a/solution.py
+++ b/solution.py
@@ -162,6 +162,8 @@
         return pl.ds(pl.multiple_of(block * T, 16), T)
 
     def cols(block, width):
+        if isinstance(block, int):
+            return pl.ds(block * width, width)
         return pl.ds(pl.multiple_of(block * width, 128), width)
 
     stage = [
@@ -310,23 +312,36 @@
     relay(Z - 1)
     for k in range(1, Z):
         produce(k)
-    if Z > 2:
-        arrive(1)
-        hop(1, lambda c: c.start())
-    for h in range(H):
-        c = pl.ds(h * HEAD_DIM, HEAD_DIM)
-        for k in range(Z - 1, 0, -1):
-            start(
-                psend.at[k - 1, :, c], part.at[z, :, c],
-                p_s.at[k, h], p_r.at[z, h], {"shard": imgs[k]},
-            )
-    gx_wait(z, core, 1)
-    gx_wait(z, diag, 2)
+
+    def chain(h, here, d, ahead, first):
+        c = cols(h, HEAD_DIM)
+        mine_k = (d - here) % Z - 1
+        if not first:
+            remote(
+                part.at[d, :, c], part.at[d, :, c], p_s.at[d, h], p_r.at[d, h], {"shard": ahead}
+            ).wait_recv()
+            psend[mine_k, :, c] = (
+                psend[mine_k, :, c].astype(jnp.float32) + part[d, :, c].astype(jnp.float32)
+            ).astype(jnp.bfloat16)
+        slot = Z if ahead == d and ahead < here else d
+        remote(
+            psend.at[mine_k, :, c], part.at[slot, :, c], p_s.at[d, h], p_r.at[slot, h],
+            {"shard": ahead},
+        ).start()
+
+    def rounds(r, h):
+        @pl.when(z == r)
+        def _():
+            for d in range(Z - 1, r, -1):
+                chain(h, r, d, r + 1, r == 0)
+
+        @pl.when(z == Z - 1 - r)
+        def _():
+            for d in range(Z - 1 - r):
+                chain(h, Z - 1 - r, d, Z - 2 - r, r == 0)
 
     def store_own(r, n, v):
         own[r:r + n, :] = v
-
-    partial(z, store_own)
 
     def weight_grad(i):
         ob_i, ob_t = split(every, i)
@@ -335,8 +350,6 @@
         dt = lax.dot_general(ob_t, g_t, TN, preferred_element_type=jnp.float32)
         return di, dt
 
-    dw_img[...], dw_txt[...] = weight_grad(z)
-
     def d_copy(h, n, t):
         return remote(
             dbuf.at[:, rows(t), cols(h, HEAD_DIM)],
@@ -344,16 +357,19 @@
             d_s.at[h, n], d_r.at[h, n], {"seq": t},
         )
 
-    def backward(h, carry):
+    def backward(h):
         c = cols(h, HEAD_DIM)
-        total = own[:, c]
-        for k in range(1, Z):
-            i = imgs[k]
-            remote(
-                part.at[i, :, c], part.at[i, :, c], p_s.at[k, h], p_r.at[i, h], {"shard": i}
-            ).wait_recv()
-            total = total + part[i, :, c].astype(jnp.float32)
-        dout = total.astype(jnp.bfloat16)
+        for slot, ok in ((z, z > 0), (Z, z < Z - 1)):
+
+            @pl.when(ok)
+            def _():
+                remote(
+                    part.at[slot, :, c], part.at[slot, :, c],
+                    p_s.at[0, h], p_r.at[slot, h], {"shard": imgs[1]},
+                ).wait_recv()
+                own[:, c] += part[slot, :, c].astype(jnp.float32)
+
+        dout = own[:, c].astype(jnp.bfloat16)
         probs = probs_s[h]
         dprobs = lax.dot_general(dout, heads[2, :, c], NT, preferred_element_type=jnp.float32)
         delta = jnp.sum(dout.astype(jnp.float32) * o_s[:, c], axis=-1, keepdims=True)
@@ -368,14 +384,27 @@
         dbuf[2, :, c] = dv.astype(jnp.bfloat16)
         for n, t in ((1, cross), (2, diag), (0, core)):
             d_copy(h, n, t).start()
-        return carry
-
-    half = (H + 1) // 2
-    lax.fori_loop(0, half, backward, 0)
-    for distance in range(2, Z - 1):
-        arrive(distance)
-        hop(distance, lambda c: c.start())
-    lax.fori_loop(half, H, backward, 0)
+
+    half = (H - 1) // 2
+    for step in range(H + Z - 1):
+        for r in range(Z - 1):
+            if 0 <= step - r < H:
+                rounds(r, step - r)
+        if step == 0:
+            gx_wait(z, core, 1)
+            gx_wait(z, diag, 2)
+            partial(z, store_own)
+        if step == 1:
+            if Z > 2:
+                arrive(1)
+                hop(1, lambda c: c.start())
+            dw_img[...], dw_txt[...] = weight_grad(z)
+        if step >= Z - 1:
+            backward(step - Z + 1)
+        if step - Z + 1 == half:
+            for distance in range(2, Z - 1):
+                arrive(distance)
+                hop(distance, lambda c: c.start())
     mine_d = pltpu.make_async_copy(dbuf.at[:, rows(s)], rbuf.at[:, :, cols(s, W)], local_sem.at[6])
     mine_d.start()
     for distance in range(max(1, Z - 1), Z):
@@ -408,6 +437,13 @@
         c.wait_send()
     for distance in range(Z - 1):
         hop(distance, lambda c: c.wait_send())
+    for k in range(1, Z):
+        for h in range(H):
+            c = cols(h, HEAD_DIM)
+            remote(
+                psend.at[k - 1, :, c], part.at[0, :, c],
+                p_s.at[imgs[k], h], p_r.at[0, h], {"shard": imgs[k]},
+            ).wait_send()
     for c in last:
         c.wait()
 
@@ -438,13 +474,13 @@
         out_specs=(hbm, hbm, vm, vm),
         scratch_shapes=[
             V((T, width), bf), V((3, T, HDW), bf), V((3, N, W), bf), V((Z, N, C), bf),
-            V((Z - 1, N, W), bf), V((Z, N, W), bf), V((N, W), f4), V((H, N, N), f4),
+            V((Z - 1, N, W), bf), V((Z + 1, N, W), bf), V((N, W), f4), V((H, N, N), f4),
             V((N, W), f4), V((Z, N, W), bf), V((3, N, W), bf), V((3, T, HDW), bf),
             D((7,)), D((Z,)), D((Z,)), D((Z, 3)), D((Z, 3)), D((S,)), D((S,)),
-            D((Z, H)), D((Z, H)), D((Z, 2)), D((Z,)), D((H, 3)), D((H, 3)),
+            D((Z, H)), D((Z + 1, H)), D((Z, 2)), D((Z,)), D((H, 3)), D((H, 3)),
         ],
         compiler_params=pltpu.CompilerParams(
-            collective_id=0, has_side_effects=True, vmem_limit_bytes=52 * 1024 * 1024
+            collective_id=0, has_side_effects=True, vmem_limit_bytes=60 * 1024 * 1024
         ),
     )(qkv_img, qkv_txt, grad_img, grad_txt, out_w_img, out_w_txt)
 

time: 142 us -> 126 us (0.89)
  Pallas kernels: 132 us -> 118 us
  local copies, waits for them, and re-layouts: 9.59 us -> 6.66 us
    pallas_call x1, Pallas kernels: 132 us -> 118 us  [fused(): pl.pallas_call(functools.partial(fused_kernel, S, Z, text), out_shape=(ja...]
    unnamed x14 -> x10, local copies, waits for them, and re-layouts: 9.59 us -> 6.66 us
where the time goes in v4:
time: 126 us; the launch traced here: 125 us
  Pallas kernels  118 us (94%)
  local copies, waits for them, and re-layouts  6.66 us (5%)
    pallas_call x1, Pallas kernels, fused(): pl.pallas_call(functools.partial(fused_kernel, S, Z, text), out_shape=(ja...  118 us
    unnamed x10, local copies, waits for them, and re-layouts  6.66 us

profile of v4, /device:TPU:0, one launch (start us, length us, event | category | flops | bytes accessed | tf_op | source)
XLA Modules:
  0.0 125.2 jit_solution(6354547962634596958)
XLA Ops:
  0.6 117.9 %shard_map.93 = (bf16[3,1,128,2048]{3,2,1,0:T(8,128)(2,1)}, bf16[3,1,16,2048]{3,2,1,0:T(8,128)(2,1)}, f32[512,768]{1,0:T(8,128)}, f32[512,768]{1,0:T(8,128)}) custom-call(bf16[3,1,128,2048]{3,2,1,0:T(8,128)(2,1)} %qkv_img.1, bf16[3,1,16,2048]{3,2,1,0:T(8,128)(2,1)} %qkv_txt.1, bf16[1,128,3072]{2,1,0:T(8,128)(2,1)} %grad_img.1, ...), custom_call_target="tpu_custom_call" | custom-call | tf_op jit(solution)/shard_map/pallas_call | solution.py:465
  118.6 0.0 copy-start.2
  118.6 0.0 copy-start.1
  118.6 2.9 %copy.14 = bf16[3,1,128,2048]{3,2,1,0:T(8,128)(2,1)} copy(bf16[3,1,128,2048]{3,2,1,0:T(8,128)(2,1)} %get-tuple-element.8) | data formatting | bytes 3145728
  121.4 0.0 copy-done.2
  121.4 0.7 copy.15
  122.1 0.0 copy-done.1
  122.1 0.0 copy-start
  122.1 1.1 copy.16
  123.3 0.8 copy-done
  124.1 1.1 copy.17
Async XLA Ops:
  118.6 2.9 %copy-start.2 = (bf16[3,1,16,2048]{3,2,1,0:T(8,128)(2,1)S(1)}, bf16[3,1,16,2048]{3,2,1,0:T(8,128)(2,1)}, u32[]{:S(2)}) copy-start(bf16[3,1,16,2048]{3,2,1,0:T(8,128)(2,1)} %get-tuple-element.9) | copy-start | bytes 589828
  118.6 3.5 %copy-start.1 = (f32[512,768]{1,0:T(8,128)S(1)}, f32[512,768]{1,0:T(8,128)}, u32[]{:S(2)}) copy-start(f32[512,768]{1,0:T(8,128)} %get-tuple-element.10) | copy-start | bytes 4718596
  122.1 2.0 %copy-start = (f32[512,768]{1,0:T(8,128)S(1)}, f32[512,768]{1,0:T(8,128)}, u32[]{:S(2)}) copy-start(f32[512,768]{1,0:T(8,128)} %get-tuple-element.11) | copy-start | bytes 4718596

commit v5 on v4

--- a/solution.py
+++ b/solution.py
@@ -309,9 +309,10 @@
         if k < Z - 1:
             relay(k)
     hop(0, lambda c: c.start())
+    for k in range(1, Z - 1):
+        produce(k)
     relay(Z - 1)
-    for k in range(1, Z):
-        produce(k)
+    produce(Z - 1)
 
     def chain(h, here, d, ahead, first):
         c = cols(h, HEAD_DIM)

time: 126 us -> 126 us (level)
  no operation moved by 1% of the time
where the time goes in v5:
time: 126 us; the launch traced here: 125 us
  Pallas kernels  118 us (94%)
  local copies, waits for them, and re-layouts  6.66 us (5%)
    pallas_call x1, Pallas kernels, fused(): pl.pallas_call(functools.partial(fused_kernel, S, Z, text), out_shape=(ja...  118 us
    unnamed x10, local copies, waits for them, and re-layouts  6.66 us

profile of v5, /device:TPU:0, one launch (start us, length us, event | category | flops | bytes accessed | tf_op | source)
XLA Modules:
  0.0 125.2 jit_solution(8852008494655766432)
XLA Ops:
  0.6 117.9 %shard_map.93 = (bf16[3,1,128,2048]{3,2,1,0:T(8,128)(2,1)}, bf16[3,1,16,2048]{3,2,1,0:T(8,128)(2,1)}, f32[512,768]{1,0:T(8,128)}, f32[512,768]{1,0:T(8,128)}) custom-call(bf16[3,1,128,2048]{3,2,1,0:T(8,128)(2,1)} %qkv_img.1, bf16[3,1,16,2048]{3,2,1,0:T(8,128)(2,1)} %qkv_txt.1, bf16[1,128,3072]{2,1,0:T(8,128)(2,1)} %grad_img.1, ...), custom_call_target="tpu_custom_call" | custom-call | tf_op jit(solution)/shard_map/pallas_call | solution.py:466
  118.6 0.0 copy-start.2
  118.6 0.0 copy-start.1
  118.6 2.9 %copy.14 = bf16[3,1,128,2048]{3,2,1,0:T(8,128)(2,1)} copy(bf16[3,1,128,2048]{3,2,1,0:T(8,128)(2,1)} %get-tuple-element.8) | data formatting | bytes 3145728
  121.4 0.0 copy-done.2
  121.4 0.7 copy.15
  122.1 0.0 copy-done.1
  122.1 0.0 copy-start
  122.1 1.1 copy.16
  123.3 0.8 copy-done
  124.1 1.1 copy.17
Async XLA Ops:
  118.6 2.9 %copy-start.2 = (bf16[3,1,16,2048]{3,2,1,0:T(8,128)(2,1)S(1)}, bf16[3,1,16,2048]{3,2,1,0:T(8,128)(2,1)}, u32[]{:S(2)}) copy-start(bf16[3,1,16,2048]{3,2,1,0:T(8,128)(2,1)} %get-tuple-element.9) | copy-start | bytes 589828
  118.6 3.5 %copy-start.1 = (f32[512,768]{1,0:T(8,128)S(1)}, f32[512,768]{1,0:T(8,128)}, u32[]{:S(2)}) copy-start(f32[512,768]{1,0:T(8,128)} %get-tuple-element.10) | copy-start | bytes 4718596
  122.1 2.0 %copy-start = (f32[512,768]{1,0:T(8,128)S(1)}, f32[512,768]{1,0:T(8,128)}, u32[]{:S(2)}) copy-start(f32[512,768]{1,0:T(8,128)} %get-tuple-element.11) | copy-start | bytes 4718596
